TPU v7x, 32 devices: a whole 2x2x4 slice. The times are simulated.
32 devices in a mesh: blk: 16 (over z, y, x), grp: 2 (over core).
Axes of the slice: x: 2, y: 2, z: 4, core: 2. Of those that a mesh axis runs over, the one named last changes fastest.
Arguments:
- samples: float32 [32, 1024], P(None, ('blk', 'grp')), may hold values from 0 to 256
- bounds: int32 [2, 32, 2048], P(None, None, 'blk'), may hold values from 0 to 256, as said below
- spread: float32 [32], replicated, may hold values from 2 to 8
- counts: int32 [2048], P('blk'), may hold values from 0 to 2047
Outputs:
- log_estimate: float32 [2048], P('blk')
- spread_grad: float32 [32], replicated
Inputs may be any that keep to these rules, and one draw needn't show every extreme that they name: For every query and dimension bounds[0] < bounds[1]; each query restricts exactly 3 dimensions to a width of 16 to 48 cells and has bounds 0 and 256 in all others.
All inputs are finite; a program needn't handle non-finite values.
Results may differ from a plain program's by a relative error of at most 0.0003.
Values sent between devices are 32-bit elements; how exact they have to be, the bound alone decides.
No kernel may reach another device: no remote copies, remote signals or barrier semaphores. Data moves between devices by JAX's collectives and lax.ppermute only.
A program may use at most 64 MiB of HBM per device.

v0:
```python
import math

import jax
import jax.numpy as jnp
from jax import lax
from jax.sharding import PartitionSpec as P

TABLE_ROWS = 1048576


root_half = 0.7071067811865476
density_norm = 0.3989422804014327


def box_terms(lower_edge, upper_edge, points, inverse):
    upper_arg = (upper_edge - points) * inverse
    lower_arg = (lower_edge - points) * inverse
    in_box = 0.5 * (lax.erf(upper_arg * root_half) - lax.erf(lower_arg * root_half))
    slopes = density_norm * (
        lower_arg * jnp.exp(-0.5 * lower_arg * lower_arg)
        - upper_arg * jnp.exp(-0.5 * upper_arg * upper_arg)
    )
    prefix_prod = jnp.cumprod(in_box, axis=0)
    behind = jnp.flip(jnp.cumprod(jnp.flip(in_box, 0), axis=0), 0)
    unit_row = jnp.ones_like(in_box[:1])
    before = jnp.concatenate([unit_row, prefix_prod[:-1]], 0)
    after_dims = jnp.concatenate([behind[1:], unit_row], 0)
    return (prefix_prod[-1], before * after_dims * slopes)


def finish(est_sum, counts_float, sample_total, query_total):
    smoothing = 1.0 / TABLE_ROWS
    estimate = est_sum / sample_total
    log_est = jnp.log(estimate + smoothing)
    target = jnp.log(counts_float / TABLE_ROWS + smoothing)
    weight = 2.0 * (log_est - target) / (query_total * (estimate + smoothing))
    return (log_est, weight)


def on_device(samples, bounds, spread, counts):
    inverse = 1.0 / spread
    lower_edge = bounds[0].astype(jnp.float32)
    upper_edge = bounds[1].astype(jnp.float32)
    dims = samples.shape[0]
    local_queries = bounds.shape[2]
    sample_total = samples.shape[1] * lax.axis_size("blk") * lax.axis_size("grp")
    query_total = local_queries * lax.axis_size("blk")
    initial = (
        jnp.zeros((local_queries,), jnp.float32),
        jnp.zeros((dims, local_queries), jnp.float32),
    )
    piece = lax.all_gather(samples, "blk", axis=1, tiled=True)
    row_count = piece.shape[1]
    width_rows = math.gcd(row_count, 32)
    blocks = piece.reshape(dims, row_count // width_rows, width_rows).transpose(1, 0, 2)

    def advance(inner, points):
        totals, gradients = box_terms(
            lower_edge[:, :, None],
            upper_edge[:, :, None],
            points[:, None, :],
            inverse[:, None, None],
        )
        return ((inner[0] + totals.sum(axis=1), inner[1] + gradients.sum(axis=2)), None)

    est_sum, grad_sum = lax.scan(advance, initial, blocks)[0]
    est_sum, grad_sum = lax.psum((est_sum, grad_sum), "grp")
    log_est, weight = finish(est_sum, counts.astype(jnp.float32), sample_total, query_total)
    share = jnp.dot(grad_sum, weight, precision=lax.Precision.HIGHEST) / sample_total
    gradient = lax.psum(share, "blk")
    return (log_est, gradient)


def solution(mesh):
    return jax.shard_map(
        on_device,
        mesh=mesh,
        in_specs=(P(None, ("blk", "grp")), P(None, None, "blk"), P(), P("blk")),
        out_specs=(P("blk"), P()),
        check_vma=False,
    )
```

profile of v0, /device:TPU:0, one launch (start us, length us, event | category | flops | bytes accessed | tf_op | source)
XLA Modules:
  0.0 137.4 jit_solution(4533394434023458910)
XLA Ops:
  1.3 0.8 copy.7
  2.1 43.8 %all_gather.3 = f32[32,512]{0,1:T(8,128)S(1)} all-gather(f32[32,32]{0,1:T(8,128)S(1)} %copy.7), channel_id=1, replica_groups=mesh['blk'=16,'grp'=2] {'blk'}, dimensions={1}, use_global_device_ids=true | all-gather | bytes 69632 | tf_op jit(solution)/shard_map/all_gather | solution.py:52
  45.9 49.9 %while.13 = (s32[]{:T(128)}, f32[128]{0:T(128)S(1)}, f32[32,128]{1,0:T(8,128)S(1)}, f32[32,128]{1,0:T(8,128)S(1)}, f32[16,32,32]{1,2,0:T(8,128)S(1)}, /*index=5*...) while((s32[]{:T(128)}, f32[128]{0:T(128)S(1)}, f32[32,128]{1,0:T(8,128)S(1)}, ...), condition=%wide.region_5.6_spmd.clone, body=%wide.region_0.5_spmd.clone.sunk | while | flops 12198019 | bytes 10025512 | solution.py:66
  46.3 0.8 copy-done
  47.5 1.0 slice-done
  49.4 0.8 copy-done
  50.6 1.0 slice-done
  53.8 1.0 slice-done
  56.9 1.0 slice-done
  60.0 1.0 slice-done
  63.1 1.0 slice-done
  66.2 1.0 slice-done
  69.4 1.0 slice-done
  72.5 1.0 slice-done
  75.6 1.0 slice-done
  78.7 1.0 slice-done
  81.8 1.0 slice-done
  83.7 0.8 copy-done
  85.0 1.0 slice-done
  88.1 1.0 slice-done
  91.2 1.0 slice-done
  94.3 1.0 slice-done
  95.8 3.4 %all-reduce.2 = (f32[128]{0:T(128)S(1)}, f32[32,128]{1,0:T(8,128)S(1)}) all-reduce(f32[128]{0:T(128)S(1)} %get-tuple-element.40, f32[32,128]{1,0:T(8,128)S(1)} %get-tuple-element.41), channel_id=1, replica_groups=mesh['blk'=16,'grp'=2] {'grp'}, use_global_device_ids=true, to_apply=%region_6.7 | all-reduce | flops 4224 | bytes 33792 | tf_op jit(solution)/shard_map/psum | solution.py:67
  100.4 37.0 %psum.23 = f32[32]{0:T(128)} all-reduce(f32[32]{0:T(128)S(1)} %fusion.18), channel_id=1, replica_groups=mesh['blk'=16,'grp'=2] {'blk'}, use_global_device_ids=true, to_apply=%region_8.9 | all-reduce | flops 32 | bytes 256 | tf_op jit(solution)/shard_map/psum | solution.py:70
  (251 shorter events, 32.1 us)
Async XLA Ops:
  0.6 1.4 %copy-start.1 = (s32[2,32,128]{2,1,0:T(8,128)S(1)}, s32[2,32,128]{2,1,0:T(8,128)}, u32[]{:S(2)}) copy-start(s32[2,32,128]{2,1,0:T(8,128)} %param.7) | copy-start | bytes 98308
  46.2 0.8 copy-start
  47.5 1.0 slice-start
  49.4 0.8 copy-start
  50.6 1.0 slice-start
  53.7 1.0 slice-start
  55.6 0.8 copy-start
  56.8 1.0 slice-start
  58.7 0.8 copy-start
  59.9 1.0 slice-start
  63.1 1.0 slice-start
  65.0 0.8 copy-start
  66.2 1.0 slice-start
  68.1 0.8 copy-start
  69.3 1.0 slice-start
  72.4 1.0 slice-start
  74.3 0.8 copy-start
  75.5 1.0 slice-start
  78.7 1.0 slice-start
  81.8 1.0 slice-start
  84.9 1.0 slice-start
  88.0 1.0 slice-start
  91.1 1.0 slice-start
  94.3 1.0 slice-start
  (12 other events, 8.9 us)
where the time goes:
time: 138 us; the launch traced here: 137 us
  blocking collectives  84.2 us (61%)
  local copies, waits for them, and re-layouts  33.4 us (24%)
  other arithmetic  17.5 us (13%)
  loops' own time  1.54 us (1%)
    all_gather x1, blocking collectives, on_device(): piece = lax.all_gather(samples, 'blk', axis=1, tiled=True)  43.8 us
    psum x1, blocking collectives, on_device(): gradient = lax.psum(share, 'blk')  37 us
    slice x32, local copies, waits for them, and re-layouts, box_terms(): before = jnp.concatenate([unit_row, prefix_prod[:-1]], 0)  15.8 us
    while x32, local copies, waits for them, and re-layouts  12.2 us
    reduce_sum x16, other arithmetic, advance(): gradients.sum(axis=2)  7.12 us
    another operation x16, other arithmetic, box_terms(): prefix_prod = jnp.cumprod(in_box, axis=0)  4.61 us
    sub x16, other arithmetic, box_terms(): lax.erf(upper_arg * root_half) - lax.erf(lower_arg * root_half)  4.29 us
    psum x1, blocking collectives, on_device(): est_sum, grad_sum = lax.psum((est_sum, grad_sum), 'grp')  3.41 us

commit v1 on v0

v1 whole, which is shorter than its diff:
```python
import functools

import jax
import jax.numpy as jnp
from jax import lax
from jax.experimental import pallas as pl
from jax.experimental.pallas import tpu as pltpu
from jax.sharding import PartitionSpec as P

TABLE_ROWS = 1048576
GRID = 256
LIMITED = 3

UNIT = 0.8493218002880191
SLOPE = 0.46971863934982566
TAIL = 0.3249638315990299
POLY = (
    0.11762449816157808,
    0.04671723593777996,
    0.3221625534171999,
    -0.31387568659162657,
    0.4408243890588848,
    -0.11345299389012899,
)


def end_terms(v):
    bell = jnp.exp2(-(v * v))
    t = pl.reciprocal(1.0 + TAIL * jnp.abs(v))
    poly = POLY[-1]
    for factor in POLY[-2::-1]:
        poly = poly * t + factor
    half = 0.5 - poly * t * bell
    return jnp.where(v < 0, -half, half), v * bell


def box_terms(low, high):
    low_erf, low_bell = end_terms(low)
    high_erf, high_bell = end_terms(high)
    return high_erf - low_erf, SLOPE * (low_bell - high_bell)


def split(x, parts):
    out = []
    for _ in range(parts - 1):
        head = x.astype(jnp.bfloat16)
        out.append(head)
        x = x - head.astype(jnp.float32)
    return out + [x.astype(jnp.bfloat16)]


def tree_sum(parts):
    while len(parts) > 1:
        parts = [a + b for a, b in zip(parts[::2], parts[1::2])]
    return parts[0]


def pack_kernel(x_ref, out_ref):
    rows, width = x_ref.shape
    out_ref[...] = jnp.concatenate(
        [x_ref[8 * j : 8 * (j + 1), :] for j in range(rows // 8)], axis=1
    )


def terms_kernel(width, *refs):
    block_refs, (bounds_ref, spread_ref, out_ref, picked, inside) = refs[:-5], refs[-5:]
    dims, queries = bounds_ref.shape[1:]
    total = len(block_refs) * width

    low, high = bounds_ref[0], bounds_ref[1]
    limited = (high - low) != GRID
    low, high = low.astype(jnp.float32), high.astype(jnp.float32)
    at = lax.broadcasted_iota(jnp.int32, (dims, queries), 0)
    first = jnp.min(jnp.where(limited, at, dims), axis=0, keepdims=True)
    last = jnp.max(jnp.where(limited, at, -1), axis=0, keepdims=True)
    is_first, is_last = at == first, at == last
    chosen = [is_first, limited & (at > first) & (at < last), is_last]

    row = lax.broadcasted_iota(jnp.int32, (dims, dims), 0)
    column = lax.broadcasted_iota(jnp.int32, (dims, dims), 1)
    spread = jnp.sum(jnp.where(row == column, spread_ref[...], 0.0), axis=1, keepdims=True)
    unit = UNIT / spread

    pick = lambda mask, values: jnp.sum(jnp.where(mask, values, 0.0), axis=0, keepdims=True)
    low_at = [pick(mask, low) for mask in chosen]
    high_at = [pick(mask, high) for mask in chosen]
    unit_at = [pick(mask, unit) for mask in chosen]

    x = jnp.concatenate(
        [
            jnp.concatenate([ref[:, width * j : width * (j + 1)] for ref in block_refs], axis=1)
            for j in range(dims // 8)
        ],
        axis=0,
    )
    full, full_slope = box_terms(-x * unit, (float(GRID) - x) * unit)
    ratio = full_slope / full
    left = jnp.concatenate(split(x, 3) + split(jnp.log(full), 3), axis=0)

    ones = [mask.astype(jnp.float32).astype(jnp.bfloat16) for mask in chosen]
    free = jnp.where(limited, 0.0, 1.0).astype(jnp.bfloat16)
    none = jnp.zeros_like(free)
    right = jnp.concatenate(
        [jnp.concatenate(ones + [none], axis=1)] * 3
        + [jnp.concatenate([none] * LIMITED + [free], axis=1)] * 3,
        axis=0,
    )
    picked[...] = lax.dot_general(
        left, right, (((0,), (0,)), ((), ())), preferred_element_type=jnp.float32
    )

    def advance(step, sums):
        rows = pl.ds(pl.multiple_of(step * 16, 16), 16)
        others = jnp.exp(picked[rows, LIMITED * queries :])
        mass, slope = [], []
        for k in range(LIMITED):
            points = picked[rows, k * queries : (k + 1) * queries]
            m, s = box_terms((low_at[k] - points) * unit_at[k], (high_at[k] - points) * unit_at[k])
            mass.append(m)
            slope.append(s)
        pair = others * mass[0]
        last_two = pair * mass[1]
        whole = last_two * mass[2]
        head, tail = split(whole, 2)
        inside[rows, :queries] = head
        inside[rows, queries:] = tail
        return (
            sums[0] + whole,
            sums[1] + others * mass[1] * mass[2] * slope[0],
            sums[2] + pair * mass[2] * slope[1],
            sums[3] + last_two * slope[2],
        )

    zero = jnp.zeros((16, queries), jnp.float32)
    sums = lax.fori_loop(0, total // 16, advance, (zero,) * 4, unroll=2)
    sums = [jnp.sum(s, axis=0, keepdims=True) for s in sums]

    ratio = jnp.concatenate(split(ratio, 2), axis=0)
    products = jnp.dot(ratio, inside[...], preferred_element_type=jnp.float32)
    deriv = products[:dims, :queries] + (products[dims:, :queries] + products[:dims, queries:])
    deriv = jnp.where(limited, 0.0, deriv)
    for mask, s in zip(chosen, sums[1:]):
        deriv = jnp.where(mask, s, deriv)
    out_ref[:dims, :] = deriv
    out_ref[dims:, :] = jnp.broadcast_to(sums[0], (8, queries))


def finish_kernel(sample_total, query_total, *refs):
    part_refs, (counts_ref, log_ref, share_ref) = refs[:-3], refs[-3:]
    whole = tree_sum([ref[...] for ref in part_refs])
    dims, queries = whole.shape[0] - 8, whole.shape[1]
    smoothing = 1.0 / TABLE_ROWS
    estimate = whole[dims : dims + 1] / sample_total
    log_est = jnp.log(estimate + smoothing)
    log_ref[...] = log_est
    target = jnp.log(counts_ref[...].astype(jnp.float32) / TABLE_ROWS + smoothing)
    weight = 2.0 * (log_est - target) / (query_total * (estimate + smoothing))
    terms = whole[:dims] * (weight / sample_total)
    terms = jnp.concatenate([terms, jnp.zeros((queries - dims, queries), jnp.float32)], axis=0)
    share_ref[...] = jnp.sum(terms.T, axis=0, keepdims=True)


def add_kernel(*refs):
    refs[-1][...] = tree_sum([ref[...] for ref in refs[:-1]])


def everyone(x, axis):
    size = lax.axis_size(axis)
    return [x] + [
        lax.ppermute(x, axis, [(i, i ^ offset) for i in range(size)]) for offset in range(1, size)
    ]


def call(kernel, args, outs, scratch=()):
    single = len(outs) == 1
    return pl.pallas_call(
        kernel,
        out_shape=outs[0] if single else outs,
        in_specs=[pl.BlockSpec(memory_space=pltpu.VMEM)] * len(args),
        out_specs=pl.BlockSpec(memory_space=pltpu.VMEM)
        if single
        else [pl.BlockSpec(memory_space=pltpu.VMEM)] * len(outs),
        scratch_shapes=list(scratch),
        compiler_params=pltpu.CompilerParams(vmem_limit_bytes=32 << 20),
    )(*args)


def shape(*sizes):
    return jax.ShapeDtypeStruct(sizes, jnp.float32)


def on_device(samples, bounds, spread, counts):
    dims, width = samples.shape
    queries = bounds.shape[2]
    blocks = lax.axis_size("blk")
    sample_total = width * blocks * lax.axis_size("grp")
    query_total = queries * blocks
    total = width * blocks

    packed = call(pack_kernel, [samples], [shape(8, dims * width // 8)])
    gathered = everyone(packed, "blk")
    part = call(
        functools.partial(terms_kernel, width),
        gathered + [bounds, spread.reshape(1, dims)],
        [shape(dims + 8, queries)],
        [
            pltpu.VMEM((total, (LIMITED + 1) * queries), jnp.float32),
            pltpu.VMEM((total, 2 * queries), jnp.bfloat16),
        ],
    )
    parts = everyone(part, "grp")
    log_est, share = call(
        functools.partial(finish_kernel, sample_total, query_total),
        parts + [counts.reshape(1, queries)],
        [shape(1, queries), shape(1, queries)],
    )
    gradient = call(add_kernel, everyone(share, "blk"), [shape(1, queries)])
    return log_est.reshape(queries), gradient[0, :dims]


def solution(mesh):
    return jax.shard_map(
        on_device,
        mesh=mesh,
        in_specs=(P(None, ("blk", "grp")), P(None, None, "blk"), P(), P("blk")),
        out_specs=(P("blk"), P()),
        check_vma=False,
    )
```

time: 138 us -> 66.8 us (0.48)
  blocking collectives: 84.2 us -> 0 us
  starting transfers between devices: 0 us -> 54.3 us
  local copies, waits for them, and re-layouts: 33.4 us -> 1.99 us
  other arithmetic: 17.5 us -> 0 us
  waiting for transfers between devices: 0 us -> 6.35 us
  Pallas kernels: 0 us -> 3.14 us
  loops' own time: 1.54 us -> 0 us
    ppermute x0 -> x31, starting transfers between devices: none -> 54.3 us  [everyone(): lax.ppermute(x, axis, [(i, i ^ offset) for i in range(size)])]
    all_gather x1 -> x0, blocking collectives: 43.8 us -> none  [on_device(): piece = lax.all_gather(samples, 'blk', axis=1, tiled=True)]
    psum x2 -> x0, blocking collectives: 40.5 us -> none  [the longest x1 37 us: on_device(): gradient = lax.psum(share, 'blk')]
    slice x64 -> x0, local copies, waits for them, and re-layouts: 16.9 us -> none  [the longest x32 15.8 us: box_terms(): before = jnp.concatenate([unit_row, prefix_prod[:-1]], 0)]
    while x32 -> x0, local copies, waits for them, and re-layouts: 12.2 us -> none
    reduce_sum x32 -> x0, other arithmetic: 7.44 us -> none  [the longest x16 7.12 us: advance(): gradients.sum(axis=2)]
    ppermute x0 -> x31, waiting for transfers between devices: none -> 6.35 us  [everyone(): lax.ppermute(x, axis, [(i, i ^ offset) for i in range(size)])]
    another operation x32 -> x0, other arithmetic: 5.43 us -> none  [the longest x16 4.61 us: box_terms(): prefix_prod = jnp.cumprod(in_box, axis=0)]
  transfers between devices with their start and end apart: 0 -> 31, of which waited for: 0 -> 7; matrix products, arithmetic and copies ran while one was open for 0% -> 0% of each run, Pallas kernels for 0% -> 0%
where the time goes in v1:
time: 66.8 us; the launch traced here: 66.5 us
  starting transfers between devices  54.3 us (81%)
  waiting for transfers between devices  6.35 us (10%)
  Pallas kernels  3.14 us (5%)
  local copies, waits for them, and re-layouts  1.99 us (3%)
  between operations  0.7 us (1%)
    ppermute x31, starting transfers between devices, everyone(): lax.ppermute(x, axis, [(i, i ^ offset) for i in range(size)])  54.3 us
    ppermute x31, waiting for transfers between devices, everyone(): lax.ppermute(x, axis, [(i, i ^ offset) for i in range(size)])  6.35 us
    pallas_call x4, Pallas kernels, call(): pl.pallas_call(kernel, out_shape=outs[0] if single else outs, in_specs=[p...  3.14 us
    unnamed x8, local copies, waits for them, and re-layouts  1.48 us
  transfers between devices with their start and end apart: 31, of which 7 were waited for; matrix products, arithmetic and copies ran while one was open for 0% of the time, Pallas kernels for 0%

profile of v1, /device:TPU:0, one launch (start us, length us, event | category | flops | bytes accessed | tf_op | source)
XLA Modules:
  0.0 66.5 jit_solution(14963148452631850749)
XLA Ops:
  0.6 0.7 %copy-done.1 = f32[32,32]{1,0:T(8,128)S(1)} copy-done((f32[32,32]{1,0:T(8,128)S(1)}, f32[32,32]{1,0:T(8,128)}, u32[]{:S(2)}) %copy-start.1) | copy-done | bytes 4120
  1.4 6.9 %collective-permute-start.14 = (f32[8,128]{1,0:T(8,128)S(1)}, f32[8,128]{1,0:T(8,128)S(1)}, u32[]{:S(2)}, u32[]{:S(2)}) collective-permute-start(f32[8,128]{1,0:T(8,128)S(1)} %shard_map.59.refs_0_), channel_id=1, source_target_pairs={{0,30},{2,28},{4,26},{6,24},{8,22},{10,20},{12,18},{14,16},{16,14}... | collective-permute-start | bytes 12296 | tf_op jit(solution)/shard_map/ppermute | solution.py:170
  8.5 3.6 %collective-permute-start.12 = (f32[8,128]{1,0:T(8,128)S(1)}, f32[8,128]{1,0:T(8,128)S(1)}, u32[]{:S(2)}, u32[]{:S(2)}) collective-permute-start(f32[8,128]{1,0:T(8,128)S(1)} %shard_map.59.refs_0_), channel_id=1, source_target_pairs={{0,26},{2,24},{4,30},{6,28},{8,18},{10,16},{12,22},{14,20},{16,10}... | collective-permute-start | bytes 12296 | tf_op jit(solution)/shard_map/ppermute | solution.py:170
  12.3 0.9 %collective-permute-start.10 = (f32[8,128]{1,0:T(8,128)S(1)}, f32[8,128]{1,0:T(8,128)S(1)}, u32[]{:S(2)}, u32[]{:S(2)}) collective-permute-start(f32[8,128]{1,0:T(8,128)S(1)} %shard_map.59.refs_0_), channel_id=1, source_target_pairs={{0,22},{2,20},{4,18},{6,16},{8,30},{10,28},{12,26},{14,24},{16,6},... | collective-permute-start | bytes 12296 | tf_op jit(solution)/shard_map/ppermute | solution.py:170
  13.2 3.9 %collective-permute-start.9 = (f32[8,128]{1,0:T(8,128)S(1)}, f32[8,128]{1,0:T(8,128)S(1)}, u32[]{:S(2)}, u32[]{:S(2)}) collective-permute-start(f32[8,128]{1,0:T(8,128)S(1)} %shard_map.59.refs_0_), channel_id=1, source_target_pairs={{0,20},{2,22},{4,16},{6,18},{8,28},{10,30},{12,24},{14,26},{16,4},... | collective-permute-start | bytes 12296 | tf_op jit(solution)/shard_map/ppermute | solution.py:170
  17.2 2.7 %collective-permute-start.7 = (f32[8,128]{1,0:T(8,128)S(1)}, f32[8,128]{1,0:T(8,128)S(1)}, u32[]{:S(2)}, u32[]{:S(2)}) collective-permute-start(f32[8,128]{1,0:T(8,128)S(1)} %shard_map.59.refs_0_), channel_id=1, source_target_pairs={{0,16},{2,18},{4,20},{6,22},{8,24},{10,26},{12,28},{14,30},{16,0},... | collective-permute-start | bytes 12296 | tf_op jit(solution)/shard_map/ppermute | solution.py:170
  19.9 3.3 %collective-permute-start.6 = (f32[8,128]{1,0:T(8,128)S(1)}, f32[8,128]{1,0:T(8,128)S(1)}, u32[]{:S(2)}, u32[]{:S(2)}) collective-permute-start(f32[8,128]{1,0:T(8,128)S(1)} %shard_map.59.refs_0_), channel_id=1, source_target_pairs={{0,14},{2,12},{4,10},{6,8},{8,6},{10,4},{12,2},{14,0},{16,30},{18,... | collective-permute-start | bytes 12296 | tf_op jit(solution)/shard_map/ppermute | solution.py:170
  23.8 1.3 %collective-permute-start.4 = (f32[8,128]{1,0:T(8,128)S(1)}, f32[8,128]{1,0:T(8,128)S(1)}, u32[]{:S(2)}, u32[]{:S(2)}) collective-permute-start(f32[8,128]{1,0:T(8,128)S(1)} %shard_map.59.refs_0_), channel_id=1, source_target_pairs={{0,10},{2,8},{4,14},{6,12},{8,2},{10,0},{12,6},{14,4},{16,26},{18,... | collective-permute-start | bytes 12296 | tf_op jit(solution)/shard_map/ppermute | solution.py:170
  25.8 2.5 %collective-permute-start.2 = (f32[8,128]{1,0:T(8,128)S(1)}, f32[8,128]{1,0:T(8,128)S(1)}, u32[]{:S(2)}, u32[]{:S(2)}) collective-permute-start(f32[8,128]{1,0:T(8,128)S(1)} %shard_map.59.refs_0_), channel_id=1, source_target_pairs={{0,6},{2,4},{4,2},{6,0},{8,14},{10,12},{12,10},{14,8},{16,22},{18,... | collective-permute-start | bytes 12296 | tf_op jit(solution)/shard_map/ppermute | solution.py:170
  29.3 1.0 %collective-permute-done.2.refs_3_ = f32[8,128]{1,0:T(8,128)S(1)} collective-permute-done((f32[8,128]{1,0:T(8,128)S(1)}, f32[8,128]{1,0:T(8,128)S(1)}, u32[]{:S(2)}, u32[]{:S(2)}) %collective-permute-start.2) | collective-permute-done | bytes 4128 | tf_op jit(solution)/shard_map/ppermute | solution.py:170
  30.3 1.6 %collective-permute-done.1.refs_2_ = f32[8,128]{1,0:T(8,128)S(1)} collective-permute-done((f32[8,128]{1,0:T(8,128)S(1)}, f32[8,128]{1,0:T(8,128)S(1)}, u32[]{:S(2)}, u32[]{:S(2)}) %collective-permute-start.1) | collective-permute-done | bytes 4128 | tf_op jit(solution)/shard_map/ppermute | solution.py:170
  32.4 0.8 %copy-done = s32[2,32,128]{2,1,0:T(8,128)S(1)} copy-done((s32[2,32,128]{2,1,0:T(8,128)S(1)}, s32[2,32,128]{2,1,0:T(8,128)}, u32[]{:S(2)}) %copy-start) | copy-done | bytes 32792
  33.2 2.5 %shard_map.60.refs_0_ = f32[40,128]{1,0:T(8,128)S(1)} custom-call(f32[8,128]{1,0:T(8,128)S(1)} %shard_map.59.refs_0_, f32[8,128]{1,0:T(8,128)S(1)} %collective-permute-done.refs_1_, f32[8,128]{1,0:T(8,128)S(1)} %collective-permute-done.1.refs_2_, f32[8,128]{1,0:T(8,128)S(1)} %collective-permute-done.2.refs_3_, f32[8,128]{1,0:T(8,128)S(1)} %collective-permute-done.3.refs_4_, ...), custom_call_target="tpu_custom_call" | custom-call | tf_op jit(solution)/shard_map/pallas_call | solution.py:176
  35.8 1.2 %collective-permute-done.15.refs_1_ = f32[40,128]{1,0:T(8,128)S(1)} collective-permute-done((f32[40,128]{1,0:T(8,128)S(1)}, f32[40,128]{1,0:T(8,128)S(1)}, u32[]{:S(2)}, u32[]{:S(2)}) %collective-permute-start.15) | collective-permute-done | bytes 20512 | tf_op jit(solution)/shard_map/ppermute | solution.py:170
  37.5 4.5 %collective-permute-start.30 = (f32[1,128]{1,0:T(1,128)S(1)}, f32[1,128]{1,0:T(1,128)S(1)}, u32[]{:S(2)}, u32[]{:S(2)}) collective-permute-start(f32[1,128]{1,0:T(1,128)S(1)} %get-tuple-element.5.refs_0_), channel_id=1, source_target_pairs={{0,30},{2,28},{4,26},{6,24},{8,22},{10,20},{12,18},{14,16},{16,14}... | collective-permute-start | bytes 1544 | tf_op jit(solution)/shard_map/ppermute | solution.py:170
  42.2 4.6 %collective-permute-start.28 = (f32[1,128]{1,0:T(1,128)S(1)}, f32[1,128]{1,0:T(1,128)S(1)}, u32[]{:S(2)}, u32[]{:S(2)}) collective-permute-start(f32[1,128]{1,0:T(1,128)S(1)} %get-tuple-element.5.refs_0_), channel_id=1, source_target_pairs={{0,26},{2,24},{4,30},{6,28},{8,18},{10,16},{12,22},{14,20},{16,10}... | collective-permute-start | bytes 1544 | tf_op jit(solution)/shard_map/ppermute | solution.py:170
  47.0 3.7 %collective-permute-start.25 = (f32[1,128]{1,0:T(1,128)S(1)}, f32[1,128]{1,0:T(1,128)S(1)}, u32[]{:S(2)}, u32[]{:S(2)}) collective-permute-start(f32[1,128]{1,0:T(1,128)S(1)} %get-tuple-element.5.refs_0_), channel_id=1, source_target_pairs={{0,20},{2,22},{4,16},{6,18},{8,28},{10,30},{12,24},{14,26},{16,4},... | collective-permute-start | bytes 1544 | tf_op jit(solution)/shard_map/ppermute | solution.py:170
  50.7 1.1 %collective-permute-start.24 = (f32[1,128]{1,0:T(1,128)S(1)}, f32[1,128]{1,0:T(1,128)S(1)}, u32[]{:S(2)}, u32[]{:S(2)}) collective-permute-start(f32[1,128]{1,0:T(1,128)S(1)} %get-tuple-element.5.refs_0_), channel_id=1, source_target_pairs={{0,18},{2,16},{4,22},{6,20},{8,26},{10,24},{12,30},{14,28},{16,2},... | collective-permute-start | bytes 1544 | tf_op jit(solution)/shard_map/ppermute | solution.py:170
  51.8 2.8 %collective-permute-start.23 = (f32[1,128]{1,0:T(1,128)S(1)}, f32[1,128]{1,0:T(1,128)S(1)}, u32[]{:S(2)}, u32[]{:S(2)}) collective-permute-start(f32[1,128]{1,0:T(1,128)S(1)} %get-tuple-element.5.refs_0_), channel_id=1, source_target_pairs={{0,16},{2,18},{4,20},{6,22},{8,24},{10,26},{12,28},{14,30},{16,0},... | collective-permute-start | bytes 1544 | tf_op jit(solution)/shard_map/ppermute | solution.py:170
  54.6 2.3 %collective-permute-start.22 = (f32[1,128]{1,0:T(1,128)S(1)}, f32[1,128]{1,0:T(1,128)S(1)}, u32[]{:S(2)}, u32[]{:S(2)}) collective-permute-start(f32[1,128]{1,0:T(1,128)S(1)} %get-tuple-element.5.refs_0_), channel_id=1, source_target_pairs={{0,14},{2,12},{4,10},{6,8},{8,6},{10,4},{12,2},{14,0},{16,30},{18,... | collective-permute-start | bytes 1544 | tf_op jit(solution)/shard_map/ppermute | solution.py:170
  57.5 2.4 %collective-permute-start.20 = (f32[1,128]{1,0:T(1,128)S(1)}, f32[1,128]{1,0:T(1,128)S(1)}, u32[]{:S(2)}, u32[]{:S(2)}) collective-permute-start(f32[1,128]{1,0:T(1,128)S(1)} %get-tuple-element.5.refs_0_), channel_id=1, source_target_pairs={{0,10},{2,8},{4,14},{6,12},{8,2},{10,0},{12,6},{14,4},{16,26},{18,... | collective-permute-start | bytes 1544 | tf_op jit(solution)/shard_map/ppermute | solution.py:170
  60.5 1.5 %collective-permute-start.18 = (f32[1,128]{1,0:T(1,128)S(1)}, f32[1,128]{1,0:T(1,128)S(1)}, u32[]{:S(2)}, u32[]{:S(2)}) collective-permute-start(f32[1,128]{1,0:T(1,128)S(1)} %get-tuple-element.5.refs_0_), channel_id=1, source_target_pairs={{0,6},{2,4},{4,2},{6,0},{8,14},{10,12},{12,10},{14,8},{16,22},{18,... | collective-permute-start | bytes 1544 | tf_op jit(solution)/shard_map/ppermute | solution.py:170
  62.4 1.5 %collective-permute-start.16 = (f32[1,128]{1,0:T(1,128)S(1)}, f32[1,128]{1,0:T(1,128)S(1)}, u32[]{:S(2)}, u32[]{:S(2)}) collective-permute-start(f32[1,128]{1,0:T(1,128)S(1)} %get-tuple-element.5.refs_0_), channel_id=1, source_target_pairs={{0,2},{2,0},{4,6},{6,4},{8,10},{10,8},{12,14},{14,12},{16,18},{18,... | collective-permute-start | bytes 1544 | tf_op jit(solution)/shard_map/ppermute | solution.py:170
  64.0 0.9 %collective-permute-done.18.refs_3_ = f32[1,128]{1,0:T(1,128)S(1)} collective-permute-done((f32[1,128]{1,0:T(1,128)S(1)}, f32[1,128]{1,0:T(1,128)S(1)}, u32[]{:S(2)}, u32[]{:S(2)}) %collective-permute-start.18) | collective-permute-done | bytes 544 | tf_op jit(solution)/shard_map/ppermute | solution.py:170
  (51 shorter events, 7.5 us)
Async XLA Ops:
  1.4 11.8 %collective-permute-start.14 = (f32[8,128]{1,0:T(8,128)S(1)}, f32[8,128]{1,0:T(8,128)S(1)}, u32[]{:S(2)}, u32[]{:S(2)}) collective-permute-start(f32[8,128]{1,0:T(8,128)S(1)} %shard_map.59.refs_0_), channel_id=1, source_target_pairs={{0,30},{2,28},{4,26},{6,24},{8,22},{10,20},{12,18},{14,16},{16,14}... | collective-permute-start | bytes 12296 | tf_op jit(solution)/shard_map/ppermute | solution.py:170
  8.4 8.7 %collective-permute-start.13 = (f32[8,128]{1,0:T(8,128)S(1)}, f32[8,128]{1,0:T(8,128)S(1)}, u32[]{:S(2)}, u32[]{:S(2)}) collective-permute-start(f32[8,128]{1,0:T(8,128)S(1)} %shard_map.59.refs_0_), channel_id=1, source_target_pairs={{0,28},{2,30},{4,24},{6,26},{8,20},{10,22},{12,16},{14,18},{16,12}... | collective-permute-start | bytes 12296 | tf_op jit(solution)/shard_map/ppermute | solution.py:170
  8.5 8.7 %collective-permute-start.12 = (f32[8,128]{1,0:T(8,128)S(1)}, f32[8,128]{1,0:T(8,128)S(1)}, u32[]{:S(2)}, u32[]{:S(2)}) collective-permute-start(f32[8,128]{1,0:T(8,128)S(1)} %shard_map.59.refs_0_), channel_id=1, source_target_pairs={{0,26},{2,24},{4,30},{6,28},{8,18},{10,16},{12,22},{14,20},{16,10}... | collective-permute-start | bytes 12296 | tf_op jit(solution)/shard_map/ppermute | solution.py:170
  12.1 7.8 %collective-permute-start.11 = (f32[8,128]{1,0:T(8,128)S(1)}, f32[8,128]{1,0:T(8,128)S(1)}, u32[]{:S(2)}, u32[]{:S(2)}) collective-permute-start(f32[8,128]{1,0:T(8,128)S(1)} %shard_map.59.refs_0_), channel_id=1, source_target_pairs={{0,24},{2,26},{4,28},{6,30},{8,16},{10,18},{12,20},{14,22},{16,8},... | collective-permute-start | bytes 12296 | tf_op jit(solution)/shard_map/ppermute | solution.py:170
  12.3 10.9 %collective-permute-start.10 = (f32[8,128]{1,0:T(8,128)S(1)}, f32[8,128]{1,0:T(8,128)S(1)}, u32[]{:S(2)}, u32[]{:S(2)}) collective-permute-start(f32[8,128]{1,0:T(8,128)S(1)} %shard_map.59.refs_0_), channel_id=1, source_target_pairs={{0,22},{2,20},{4,18},{6,16},{8,30},{10,28},{12,26},{14,24},{16,6},... | collective-permute-start | bytes 12296 | tf_op jit(solution)/shard_map/ppermute | solution.py:170
  13.2 10.6 %collective-permute-start.9 = (f32[8,128]{1,0:T(8,128)S(1)}, f32[8,128]{1,0:T(8,128)S(1)}, u32[]{:S(2)}, u32[]{:S(2)}) collective-permute-start(f32[8,128]{1,0:T(8,128)S(1)} %shard_map.59.refs_0_), channel_id=1, source_target_pairs={{0,20},{2,22},{4,16},{6,18},{8,28},{10,30},{12,24},{14,26},{16,4},... | collective-permute-start | bytes 12296 | tf_op jit(solution)/shard_map/ppermute | solution.py:170
  17.1 8.1 %collective-permute-start.8 = (f32[8,128]{1,0:T(8,128)S(1)}, f32[8,128]{1,0:T(8,128)S(1)}, u32[]{:S(2)}, u32[]{:S(2)}) collective-permute-start(f32[8,128]{1,0:T(8,128)S(1)} %shard_map.59.refs_0_), channel_id=1, source_target_pairs={{0,18},{2,16},{4,22},{6,20},{8,26},{10,24},{12,30},{14,28},{16,2},... | collective-permute-start | bytes 12296 | tf_op jit(solution)/shard_map/ppermute | solution.py:170
  17.2 8.6 %collective-permute-start.7 = (f32[8,128]{1,0:T(8,128)S(1)}, f32[8,128]{1,0:T(8,128)S(1)}, u32[]{:S(2)}, u32[]{:S(2)}) collective-permute-start(f32[8,128]{1,0:T(8,128)S(1)} %shard_map.59.refs_0_), channel_id=1, source_target_pairs={{0,16},{2,18},{4,20},{6,22},{8,24},{10,26},{12,28},{14,30},{16,0},... | collective-permute-start | bytes 12296 | tf_op jit(solution)/shard_map/ppermute | solution.py:170
  19.9 8.4 %collective-permute-start.6 = (f32[8,128]{1,0:T(8,128)S(1)}, f32[8,128]{1,0:T(8,128)S(1)}, u32[]{:S(2)}, u32[]{:S(2)}) collective-permute-start(f32[8,128]{1,0:T(8,128)S(1)} %shard_map.59.refs_0_), channel_id=1, source_target_pairs={{0,14},{2,12},{4,10},{6,8},{8,6},{10,4},{12,2},{14,0},{16,30},{18,... | collective-permute-start | bytes 12296 | tf_op jit(solution)/shard_map/ppermute | solution.py:170
  23.2 5.6 %collective-permute-start.5 = (f32[8,128]{1,0:T(8,128)S(1)}, f32[8,128]{1,0:T(8,128)S(1)}, u32[]{:S(2)}, u32[]{:S(2)}) collective-permute-start(f32[8,128]{1,0:T(8,128)S(1)} %shard_map.59.refs_0_), channel_id=1, source_target_pairs={{0,12},{2,14},{4,8},{6,10},{8,4},{10,6},{12,0},{14,2},{16,28},{18,... | collective-permute-start | bytes 12296 | tf_op jit(solution)/shard_map/ppermute | solution.py:170
  23.8 5.4 %collective-permute-start.4 = (f32[8,128]{1,0:T(8,128)S(1)}, f32[8,128]{1,0:T(8,128)S(1)}, u32[]{:S(2)}, u32[]{:S(2)}) collective-permute-start(f32[8,128]{1,0:T(8,128)S(1)} %shard_map.59.refs_0_), channel_id=1, source_target_pairs={{0,10},{2,8},{4,14},{6,12},{8,2},{10,0},{12,6},{14,4},{16,26},{18,... | collective-permute-start | bytes 12296 | tf_op jit(solution)/shard_map/ppermute | solution.py:170
  25.8 4.5 %collective-permute-start.2 = (f32[8,128]{1,0:T(8,128)S(1)}, f32[8,128]{1,0:T(8,128)S(1)}, u32[]{:S(2)}, u32[]{:S(2)}) collective-permute-start(f32[8,128]{1,0:T(8,128)S(1)} %shard_map.59.refs_0_), channel_id=1, source_target_pairs={{0,6},{2,4},{4,2},{6,0},{8,14},{10,12},{12,10},{14,8},{16,22},{18,... | collective-permute-start | bytes 12296 | tf_op jit(solution)/shard_map/ppermute | solution.py:170
  37.5 9.5 %collective-permute-start.30 = (f32[1,128]{1,0:T(1,128)S(1)}, f32[1,128]{1,0:T(1,128)S(1)}, u32[]{:S(2)}, u32[]{:S(2)}) collective-permute-start(f32[1,128]{1,0:T(1,128)S(1)} %get-tuple-element.5.refs_0_), channel_id=1, source_target_pairs={{0,30},{2,28},{4,26},{6,24},{8,22},{10,20},{12,18},{14,16},{16,14}... | collective-permute-start | bytes 1544 | tf_op jit(solution)/shard_map/ppermute | solution.py:170
  42.0 8.7 %collective-permute-start.29 = (f32[1,128]{1,0:T(1,128)S(1)}, f32[1,128]{1,0:T(1,128)S(1)}, u32[]{:S(2)}, u32[]{:S(2)}) collective-permute-start(f32[1,128]{1,0:T(1,128)S(1)} %get-tuple-element.5.refs_0_), channel_id=1, source_target_pairs={{0,28},{2,30},{4,24},{6,26},{8,20},{10,22},{12,16},{14,18},{16,12}... | collective-permute-start | bytes 1544 | tf_op jit(solution)/shard_map/ppermute | solution.py:170
  42.2 9.7 %collective-permute-start.28 = (f32[1,128]{1,0:T(1,128)S(1)}, f32[1,128]{1,0:T(1,128)S(1)}, u32[]{:S(2)}, u32[]{:S(2)}) collective-permute-start(f32[1,128]{1,0:T(1,128)S(1)} %get-tuple-element.5.refs_0_), channel_id=1, source_target_pairs={{0,26},{2,24},{4,30},{6,28},{8,18},{10,16},{12,22},{14,20},{16,10}... | collective-permute-start | bytes 1544 | tf_op jit(solution)/shard_map/ppermute | solution.py:170
  46.7 7.9 %collective-permute-start.27 = (f32[1,128]{1,0:T(1,128)S(1)}, f32[1,128]{1,0:T(1,128)S(1)}, u32[]{:S(2)}, u32[]{:S(2)}) collective-permute-start(f32[1,128]{1,0:T(1,128)S(1)} %get-tuple-element.5.refs_0_), channel_id=1, source_target_pairs={{0,24},{2,26},{4,28},{6,30},{8,16},{10,18},{12,20},{14,22},{16,8},... | collective-permute-start | bytes 1544 | tf_op jit(solution)/shard_map/ppermute | solution.py:170
  47.0 9.9 %collective-permute-start.26 = (f32[1,128]{1,0:T(1,128)S(1)}, f32[1,128]{1,0:T(1,128)S(1)}, u32[]{:S(2)}, u32[]{:S(2)}) collective-permute-start(f32[1,128]{1,0:T(1,128)S(1)} %get-tuple-element.5.refs_0_), channel_id=1, source_target_pairs={{0,22},{2,20},{4,18},{6,16},{8,30},{10,28},{12,26},{14,24},{16,6},... | collective-permute-start | bytes 1544 | tf_op jit(solution)/shard_map/ppermute | solution.py:170
  47.0 10.5 %collective-permute-start.25 = (f32[1,128]{1,0:T(1,128)S(1)}, f32[1,128]{1,0:T(1,128)S(1)}, u32[]{:S(2)}, u32[]{:S(2)}) collective-permute-start(f32[1,128]{1,0:T(1,128)S(1)} %get-tuple-element.5.refs_0_), channel_id=1, source_target_pairs={{0,20},{2,22},{4,16},{6,18},{8,28},{10,30},{12,24},{14,26},{16,4},... | collective-permute-start | bytes 1544 | tf_op jit(solution)/shard_map/ppermute | solution.py:170
  50.7 9.1 %collective-permute-start.24 = (f32[1,128]{1,0:T(1,128)S(1)}, f32[1,128]{1,0:T(1,128)S(1)}, u32[]{:S(2)}, u32[]{:S(2)}) collective-permute-start(f32[1,128]{1,0:T(1,128)S(1)} %get-tuple-element.5.refs_0_), channel_id=1, source_target_pairs={{0,18},{2,16},{4,22},{6,20},{8,26},{10,24},{12,30},{14,28},{16,2},... | collective-permute-start | bytes 1544 | tf_op jit(solution)/shard_map/ppermute | solution.py:170
  51.8 8.7 %collective-permute-start.23 = (f32[1,128]{1,0:T(1,128)S(1)}, f32[1,128]{1,0:T(1,128)S(1)}, u32[]{:S(2)}, u32[]{:S(2)}) collective-permute-start(f32[1,128]{1,0:T(1,128)S(1)} %get-tuple-element.5.refs_0_), channel_id=1, source_target_pairs={{0,16},{2,18},{4,20},{6,22},{8,24},{10,26},{12,28},{14,30},{16,0},... | collective-permute-start | bytes 1544 | tf_op jit(solution)/shard_map/ppermute | solution.py:170
  54.6 7.4 %collective-permute-start.22 = (f32[1,128]{1,0:T(1,128)S(1)}, f32[1,128]{1,0:T(1,128)S(1)}, u32[]{:S(2)}, u32[]{:S(2)}) collective-permute-start(f32[1,128]{1,0:T(1,128)S(1)} %get-tuple-element.5.refs_0_), channel_id=1, source_target_pairs={{0,14},{2,12},{4,10},{6,8},{8,6},{10,4},{12,2},{14,0},{16,30},{18,... | collective-permute-start | bytes 1544 | tf_op jit(solution)/shard_map/ppermute | solution.py:170
  56.9 5.5 %collective-permute-start.21 = (f32[1,128]{1,0:T(1,128)S(1)}, f32[1,128]{1,0:T(1,128)S(1)}, u32[]{:S(2)}, u32[]{:S(2)}) collective-permute-start(f32[1,128]{1,0:T(1,128)S(1)} %get-tuple-element.5.refs_0_), channel_id=1, source_target_pairs={{0,12},{2,14},{4,8},{6,10},{8,4},{10,6},{12,0},{14,2},{16,28},{18,... | collective-permute-start | bytes 1544 | tf_op jit(solution)/shard_map/ppermute | solution.py:170
  57.5 6.5 %collective-permute-start.20 = (f32[1,128]{1,0:T(1,128)S(1)}, f32[1,128]{1,0:T(1,128)S(1)}, u32[]{:S(2)}, u32[]{:S(2)}) collective-permute-start(f32[1,128]{1,0:T(1,128)S(1)} %get-tuple-element.5.refs_0_), channel_id=1, source_target_pairs={{0,10},{2,8},{4,14},{6,12},{8,2},{10,0},{12,6},{14,4},{16,26},{18,... | collective-permute-start | bytes 1544 | tf_op jit(solution)/shard_map/ppermute | solution.py:170
  60.5 4.4 %collective-permute-start.18 = (f32[1,128]{1,0:T(1,128)S(1)}, f32[1,128]{1,0:T(1,128)S(1)}, u32[]{:S(2)}, u32[]{:S(2)}) collective-permute-start(f32[1,128]{1,0:T(1,128)S(1)} %get-tuple-element.5.refs_0_), channel_id=1, source_target_pairs={{0,6},{2,4},{4,2},{6,0},{8,14},{10,12},{12,10},{14,8},{16,22},{18,... | collective-permute-start | bytes 1544 | tf_op jit(solution)/shard_map/ppermute | solution.py:170
  (11 other events, 57.6 us)
